TPU v7x, 512 devices: a whole 4x8x8 slice. The times are simulated.
512 devices in a mesh: seq: 64 (over z, x, core), mp: 8 (over y).
Axes of the slice: x: 4, y: 8, z: 8, core: 2. Of those that a mesh axis runs over, the one named last changes fastest.
Arguments:
- frames_tokens: bfloat16 [8192, 8192], P('seq', 'mp')
- positions: int32 [8192, 3], P('seq'), may hold values from 0 to 1471, as said below
- norm_gain: bfloat16 [8192], replicated, may hold values from 0.099609375 to 1.8984375
- w_query: bfloat16 [8192, 4096], P('seq', 'mp'), may hold values from -0.109375 to 0.109375
- w_key: bfloat16 [8192, 512], P('seq'), may hold values from -0.109375 to 0.109375
- w_value: bfloat16 [8192, 512], P('seq'), may hold values from -0.0625 to 0.0625
- b_query: bfloat16 [4096], P('mp')
- b_key: bfloat16 [512], replicated
- b_value: bfloat16 [512], replicated, may hold values from -3 to 3
Outputs:
- attended: bfloat16 [8192, 4096], P('seq', 'mp')
Inputs may be any that keep to these rules, and one draw needn't show every extreme that they name: Row k of positions belongs to the token in row k of frames_tokens. Tokens come in clips of whole frames; a token's ids are its frame, grid row and grid column inside its clip plus the clip's start, and each clip starts beyond every id of the clips before it.
All inputs are finite; a program needn't handle non-finite values.
Results may differ from a plain program's by a relative error of at most 0.01.
The roundings to bfloat16 on the way count: a program that leaves them out, or rounds other values in their place, can miss the bound.
Values may be sent and summed in bfloat16 or wider, within the bound.
A program may use at most 64 MiB of HBM per device.

v0:
```python
import math

import jax
import jax.numpy as jnp
from jax import lax
from jax.sharding import PartitionSpec as P

HD = 128
HQ = 32
HK = 4


def rotary_angles(rope_ids, half_dim):
    freq_index = jnp.arange(half_dim)
    frequency = jnp.power(1000000.0, -(2.0 * freq_index.astype(jnp.float32)) / (2 * half_dim))
    section = jnp.where(
        freq_index < 2 * half_dim // 8, 0, jnp.where(freq_index < 5 * 2 * half_dim // 16, 1, 2)
    )
    chosen = jnp.where(
        section[None, :] == 0,
        rope_ids[:, 0:1],
        jnp.where(section[None, :] == 1, rope_ids[:, 1:2], rope_ids[:, 2:3]),
    )
    return chosen.astype(jnp.float32) * frequency[None, :]


def rotate(linear, angles, heads):
    row_count = linear.shape[0]
    half_dim = angles.shape[1]
    halves = linear.reshape(row_count, heads, 2, half_dim)
    cosine = jnp.cos(angles)[:, None, :]
    sines = jnp.sin(angles)[:, None, :]
    front_half = halves[:, :, 0, :]
    back_half = halves[:, :, 1, :]
    turned = jnp.stack(
        [front_half * cosine - back_half * sines, back_half * cosine + front_half * sines], axis=2
    )
    return turned.reshape(row_count, heads * 2 * half_dim).astype(jnp.bfloat16)


def shards(frames_tokens, positions, norm_gain, w_query, w_key, w_value, b_query, b_key, b_value):
    seq_count = lax.axis_size("seq")
    mp_count = lax.axis_size("mp")
    row_count = frames_tokens.shape[0]
    block_len = row_count // seq_count
    seq_index = lax.axis_index("seq")
    mp_index = lax.axis_index("mp")
    row_index = jnp.arange(row_count, dtype=jnp.int32)
    moved, moved_ids = (
        lax.all_to_all(
            frames_tokens.reshape(seq_count, block_len, frames_tokens.shape[1]),
            "seq",
            split_axis=0,
            concat_axis=0,
            tiled=True,
        ),
        lax.all_to_all(
            positions.reshape(seq_count, block_len, 3),
            "seq",
            split_axis=0,
            concat_axis=0,
            tiled=True,
        ),
    )
    tokens = moved.reshape(row_count, frames_tokens.shape[1])
    rope_ids = moved_ids.reshape(row_count, 3)
    query_pos = seq_index * row_count + row_index
    gathered = lax.all_gather(tokens, "mp", axis=1, tiled=True)
    widened = gathered.astype(jnp.float32)
    inverse = lax.rsqrt(jnp.mean(widened * widened, axis=1, keepdims=True) + 1e-06)
    normed = (widened * inverse * norm_gain.astype(jnp.float32)[None, :]).astype(jnp.bfloat16)
    query_cols = w_query.shape[1]
    query_heads = query_cols // HD
    group_size = HQ // HK
    key_heads = max(1, HK // mp_count)
    first_head = mp_index * query_heads // group_size
    key_cols = key_heads * HD
    key_part = lax.dynamic_slice_in_dim(w_key, first_head * HD, key_cols, 1)
    value_part = lax.dynamic_slice_in_dim(w_value, first_head * HD, key_cols, 1)
    key_bias = lax.dynamic_slice_in_dim(b_key, first_head * HD, key_cols, 0)
    value_bias = lax.dynamic_slice_in_dim(b_value, first_head * HD, key_cols, 0)
    pieces = (
        lax.all_gather(w_query, "seq", axis=0, tiled=True),
        lax.all_gather(key_part, "seq", axis=0, tiled=True),
        lax.all_gather(value_part, "seq", axis=0, tiled=True),
    )
    query_linear, key_linear, value_linear = tuple(
        (
            jnp.dot(normed, weight_piece, preferred_element_type=jnp.float32)
            for weight_piece in pieces
        )
    )
    query_linear = query_linear + b_query.astype(jnp.float32)[None, :]
    key_linear = key_linear + key_bias.astype(jnp.float32)[None, :]
    value_linear = value_linear + value_bias.astype(jnp.float32)[None, :]
    angles = rotary_angles(rope_ids, HD // 2)
    local_group = query_heads // key_heads
    queries = rotate(query_linear, angles, query_heads).reshape(
        row_count, key_heads, local_group, HD
    )
    key_rot = rotate(key_linear, angles, key_heads)
    value_rows = value_linear.astype(jnp.bfloat16)
    softscale = 1.0 / math.sqrt(HD)
    last_query = jnp.max(query_pos)
    start_state = (
        jnp.full((row_count, key_heads, local_group), -1e30, jnp.float32),
        jnp.zeros((row_count, key_heads, local_group), jnp.float32),
        jnp.zeros((row_count, key_heads, local_group, HD), jnp.float32),
    )
    pieces = (
        lax.all_gather(key_rot, "seq", axis=0, tiled=True),
        lax.all_gather(value_rows, "seq", axis=0, tiled=True),
    )
    piece_rows = pieces[0].shape[0]
    shard_count = max(1, piece_rows // row_count)
    tile_span = 1
    for candidate in range(1, 9):
        if shard_count % candidate == 0:
            tile_span = candidate
    tile_rows = min(piece_rows, tile_span * row_count)

    def tile_step(tile_index, carry_in):
        first_row = tile_index * tile_rows
        key_pos = first_row + jnp.arange(tile_rows, dtype=jnp.int32)

        def compute(carry_now):
            running_max, denominator, weighted = carry_now
            key_tile = lax.dynamic_slice_in_dim(
                pieces[0], tile_index * tile_rows, tile_rows, 0
            ).reshape(tile_rows, key_heads, HD)
            value_tile = lax.dynamic_slice_in_dim(
                pieces[1], tile_index * tile_rows, tile_rows, 0
            ).reshape(tile_rows, key_heads, HD)
            scores = (
                jnp.einsum("qkgd,tkd->qkgt", queries, key_tile, preferred_element_type=jnp.float32)
                * softscale
            )
            visible = (key_pos[None, :] <= query_pos[:, None])[:, None, None, :]
            masked = jnp.where(visible, scores, -1e30)
            new_max = jnp.maximum(running_max, jnp.max(masked, axis=3))
            factor = jnp.exp(running_max - new_max)
            exp_terms = jnp.where(visible, jnp.exp(masked - new_max[..., None]), 0.0)
            denominator = denominator * factor + jnp.sum(exp_terms, axis=3)
            weighted = weighted * factor[..., None] + jnp.einsum(
                "qkgt,tkd->qkgd",
                exp_terms.astype(jnp.bfloat16),
                value_tile,
                preferred_element_type=jnp.float32,
            )
            return (new_max, denominator, weighted)

        return lax.cond(
            jnp.min(key_pos) > last_query, lambda keep_state: keep_state, compute, carry_in
        )

    running_max, denominator, weighted = lax.fori_loop(
        0, piece_rows // tile_rows, tile_step, start_state
    )
    attended = (
        (weighted / denominator[..., None]).reshape(row_count, query_cols).astype(jnp.bfloat16)
    )
    return attended


def solution(mesh):
    in_specs = (
        P("seq", "mp"),
        P("seq", None),
        P(),
        P("seq", "mp"),
        P("seq", None),
        P("seq", None),
        P("mp"),
        P(),
        P(),
    )
    out_specs = P("seq", "mp")
    return jax.shard_map(shards, mesh=mesh, in_specs=in_specs, out_specs=out_specs, check_vma=False)
```

profile of v0, /device:TPU:449, one launch (start us, length us, event | category | flops | bytes accessed | tf_op | source)
XLA Modules:
  0.0 545.4 jit_solution(6152464964259276686)
XLA Ops:
  7.6 19.1 %all_to_all.10 = bf16[64,2,1024]{2,1,0:T(2,128)(2,1)S(1)} all-to-all(bf16[64,2,1024]{2,1,0:T(2,128)(2,1)S(1)} %reshape.525), channel_id=1, replica_groups=mesh['seq'=64,'mp'=8] {'seq'}, dimensions={0} | all-to-all | bytes 524288 | tf_op jit(solution)/shard_map/all_to_all | solution.py:50
  31.2 6.7 %all-to-all-start.1 = ((s32[64,2,3]{2,1,0:T(2,128)}), s32[64,2,3]{2,1,0:T(2,128)S(1)}, u32[]{:S(2)}, u32[]{:S(2)}) async-start(s32[64,2,3]{2,1,0:T(2,128)} %bitcast.13), calls=%async_computation.1 | async-start | bytes 131072 | tf_op jit(solution)/shard_map/all_to_all | solution.py:57
  38.0 7.2 %all-to-all-done.1 = s32[64,2,3]{2,1,0:T(2,128)S(1)} async-done(((s32[64,2,3]{2,1,0:T(2,128)}), s32[64,2,3]{2,1,0:T(2,128)S(1)}, u32[]{:S(2)}, u32[]{:S(2)}) %all-to-all-start.1) | async-done | bytes 1568 | tf_op jit(solution)/shard_map/all_to_all | solution.py:57
  45.5 20.2 %all-gather.7.cloned.1.call-done = bf16[128,8192]{1,0:T(8,128)(2,1)} async-done(((bf16[128,1024]{1,0:T(8,128)(2,1)}), bf16[128,8192]{1,0:T(8,128)(2,1)}) %all-gather.7.cloned.1.call-update) | async-done | bytes 2097168 | tf_op jit(solution)/shard_map/all_gather | solution.py:68
  65.8 2.2 fusion.26
  68.0 85.7 %all-gather.9.cloned.1.call-done = bf16[8192,128]{1,0:T(8,128)(2,1)} async-done(((bf16[128,128]{1,0:T(8,128)(2,1)}), bf16[8192,128]{1,0:T(8,128)(2,1)}) %all-gather.9.cloned.1.call-update) | async-done | bytes 2097168 | tf_op jit(solution)/shard_map/all_gather | solution.py:84
  153.8 2.7 convolution_add_fusion.2
  157.5 80.3 %all-gather.15.cloned.1.call-done = bf16[8192,128]{1,0:T(8,128)(2,1)} async-done(((bf16[128,128]{1,0:T(8,128)(2,1)}), bf16[8192,128]{1,0:T(8,128)(2,1)}) %all-gather.15.cloned.1.call-update) | async-done | bytes 2097168 | tf_op jit(solution)/shard_map/all_gather | solution.py:85
  237.7 3.0 fusion.29
  242.3 75.0 %all-gather.11.cloned.1.call-done = bf16[8192,128]{0,1:T(8,128)(2,1)} async-done(((bf16[128,128]{0,1:T(8,128)(2,1)}), bf16[8192,128]{0,1:T(8,128)(2,1)}) %all-gather.11.cloned.1.call-update) | async-done | bytes 2097168 | tf_op jit(solution)/shard_map/all_gather | solution.py:111
  317.3 3.2 copy.25
  320.5 81.5 %all-gather.17.cloned.1.call-done = bf16[8192,128]{1,0:T(8,128)(2,1)} async-done(((bf16[128,128]{1,0:T(8,128)(2,1)}), bf16[8192,128]{1,0:T(8,128)(2,1)}) %all-gather.17.cloned.1.call-update) | async-done | bytes 2097168 | tf_op jit(solution)/shard_map/all_gather | solution.py:112
  402.0 4.1 copy.27
  406.0 85.9 %all-gather.13.cloned.1.call-done = bf16[8192,512]{1,0:T(8,128)(2,1)} async-done(((bf16[128,512]{1,0:T(8,128)(2,1)}), bf16[8192,512]{1,0:T(8,128)(2,1)}) %all-gather.13.cloned.1.call-update) | async-done | bytes 8388624 | tf_op jit(solution)/shard_map/all_gather | solution.py:83
  492.0 5.3 convolution_add_fusion
  497.7 40.1 %while.18 = (s32[]{:T(128)}, f32[128,1,4]{0,2,1:T(4,128)S(1)}, f32[128,1,4]{0,2,1:T(4,128)S(1)}, f32[128,1,4,128]{0,3,2,1:T(8,128)S(1)}, s32[]{:T(128)}, /*index...) while((s32[]{:T(128)}, f32[128,1,4]{0,2,1:T(4,128)S(1)}, ...), condition=%wide.region_8.9_spmd.clone, body=%wide.region_2.8_spmd.clone.sunk | while | flops 275517056 | bytes 8038737 | solution.py:156
  499.7 2.9 conditional.3
  501.0 1.6 fusion.5
  504.8 2.9 conditional.3
  506.0 1.6 fusion.5
  509.8 2.9 conditional.3
  511.0 1.6 fusion.5
  514.8 2.9 conditional.3
  516.0 1.6 fusion.5
  519.8 2.9 conditional.3
  521.0 1.6 fusion.5
  524.8 2.9 conditional.3
  526.1 1.6 fusion.5
  529.8 2.9 conditional.3
  531.1 1.6 fusion.5
  534.8 2.9 conditional.3
  536.1 1.6 fusion.5
  (125 shorter events, 24.9 us)
Async XLA Ops:
  6.5 21.1 %copy-start = (bf16[128,512]{1,0:T(8,128)(2,1)S(1)}, bf16[128,512]{1,0:T(8,128)(2,1)}, u32[]{:S(2)}) copy-start(bf16[128,512]{1,0:T(8,128)(2,1)} %param.17) | copy-start | bytes 393220
  6.5 31.4 %copy-start.4 = (bf16[512]{0:T(512)(128)(2,1)S(1)}, bf16[512]{0:T(512)(128)(2,1)}, u32[]{:S(2)}) copy-start(bf16[512]{0:T(512)(128)(2,1)} %param.20) | copy-start | bytes 3076
  6.5 31.5 %copy-start.2 = (bf16[8192]{0:T(1024)(128)(2,1)S(1)}, bf16[8192]{0:T(1024)(128)(2,1)}, u32[]{:S(2)}) copy-start(bf16[8192]{0:T(1024)(128)(2,1)} %param.15) | copy-start | bytes 49156
  6.5 59.2 %all-gather.7.cloned.1.call-start = ((), (), s32[]{:S(2)}) async-start(), calls=%async_computation.2 | async-start | bytes 2359296 | tf_op jit(solution)/shard_map/all_gather | solution.py:68
  27.6 126.2 %all-gather.9.cloned.1.call-start = ((), (), s32[]{:S(2)}) async-start(), calls=%async_computation.3 | async-start | bytes 2129920 | tf_op jit(solution)/shard_map/all_gather | solution.py:84
  28.3 209.4 %all-gather.15.cloned.1.call-start = ((), (), s32[]{:S(2)}) async-start(), calls=%async_computation.6 | async-start | bytes 2129920 | tf_op jit(solution)/shard_map/all_gather | solution.py:85
  31.2 14.0 %all-to-all-start.1 = ((s32[64,2,3]{2,1,0:T(2,128)}), s32[64,2,3]{2,1,0:T(2,128)S(1)}, u32[]{:S(2)}, u32[]{:S(2)}) async-start(s32[64,2,3]{2,1,0:T(2,128)} %bitcast.13), calls=%async_computation.1 | async-start | bytes 131072 | tf_op jit(solution)/shard_map/all_to_all | solution.py:57
  37.9 279.4 %all-gather.11.cloned.1.call-start = ((), (), s32[]{:S(2)}) async-start(), calls=%async_computation.4 | async-start | bytes 2129920 | tf_op jit(solution)/shard_map/all_gather | solution.py:111
  65.8 88.0 %copy-start.1 = (bf16[128,8192]{1,0:T(8,128)(2,1)S(1)}, bf16[128,8192]{1,0:T(8,128)(2,1)}, u32[]{:S(2)}) copy-start(bf16[128,8192]{1,0:T(8,128)(2,1)} %all-gather.7.cloned.1.call-done) | copy-start | bytes 6291460
  68.0 89.3 %copy-start.5 = (bf16[512]{0:T(512)(128)(2,1)S(1)}, bf16[512]{0:T(512)(128)(2,1)}, u32[]{:S(2)}) copy-start(bf16[512]{0:T(512)(128)(2,1)} %param.21) | copy-start | bytes 3076
  157.3 244.6 %all-gather.17.cloned.1.call-start = ((), (), s32[]{:S(2)}) async-start(), calls=%async_computation.7 | async-start | bytes 2129920 | tf_op jit(solution)/shard_map/all_gather | solution.py:112
  157.5 84.6 %copy-start.3 = (bf16[512]{0:T(512)(128)(2,1)S(1)}, bf16[512]{0:T(512)(128)(2,1)}, u32[]{:S(2)}) copy-start(bf16[512]{0:T(512)(128)(2,1)} %param.19) | copy-start | bytes 3076
  240.8 251.2 %all-gather.13.cloned.1.call-start = ((), (), s32[]{:S(2)}) async-start(), calls=%async_computation.5 | async-start | bytes 8519680 | tf_op jit(solution)/shard_map/all_gather | solution.py:83
Sparse Core Ops, SparseCore 0:
  27.7 38.0 all-gather.6
  69.1 84.5 all-gather.8
  157.1 80.5 all-gather.14
  240.8 76.3 all-gather.10
  320.5 81.4 all-gather.16
  405.2 86.7 all-gather.12
where the time goes:
time: 546 us; the launch traced here: 545 us
  waiting for transfers between devices  436 us (80%)
  matrix products  27.6 us (5%)
  blocking collectives  19.1 us (3%)
  other arithmetic  16 us (3%)
  local copies, waits for them, and re-layouts  14 us (3%)
  between operations  13.7 us (3%)
  loops' own time  11.7 us (2%)
  starting transfers between devices  6.9 us (1%)
    all_gather x1, waiting for transfers between devices, shards(): lax.all_gather(w_query, 'seq', axis=0, tiled=True)  85.9 us
    all_gather x1, waiting for transfers between devices, shards(): lax.all_gather(key_part, 'seq', axis=0, tiled=True)  85.7 us
    all_gather x1, waiting for transfers between devices, shards(): lax.all_gather(value_rows, 'seq', axis=0, tiled=True)  81.5 us
    all_gather x1, waiting for transfers between devices, shards(): lax.all_gather(value_part, 'seq', axis=0, tiled=True)  80.3 us
    all_gather x1, waiting for transfers between devices, shards(): lax.all_gather(key_rot, 'seq', axis=0, tiled=True)  75 us
    all_gather x1, waiting for transfers between devices, shards(): gathered = lax.all_gather(tokens, 'mp', axis=1, tiled=True)  20.2 us
    all_to_all x1, blocking collectives, shards(): lax.all_to_all(frames_tokens.reshape(seq_count, block_len, frames_tokens....  19.1 us
    dot_general x8, matrix products, compute(): jnp.einsum('qkgt,tkd->qkgd', exp_terms.astype(jnp.bfloat16), value_tile,...  13.1 us
  transfers between devices with their start and end apart: 7, of which 7 were waited for; matrix products, arithmetic and copies ran while one was open for 4% of the time, Pallas kernels for 0%

commit v1 on v0

v1 whole, which is shorter than its diff:
```python
import functools
import math

import jax
import jax.numpy as jnp
import numpy as np
from jax import lax
from jax.experimental import pallas as pl
from jax.experimental.pallas import tpu as pltpu
from jax.sharding import PartitionSpec as P

HD = 128
T = 128
NX, NZ, NM = 4, 8, 8
NS = NZ * NX * 2
CA, CB = 256, 384
MESH = pl.DeviceIdType.MESH
DIST = [[0], [-1, 1], [-2, 2], [-3, 3], [4]]
EXP_SCALE = math.log2(math.e) / math.sqrt(HD)


class Gather:
    def __init__(self, a, b, sems, z, x, c, m):
        self.a, self.b = a, b
        self.ra, self.rb, self.ca, self.cb, self.sza, self.sxa, self.szb, self.sxb, self.sca, self.scb = sems
        self.z, self.x, self.c, self.m = z, x, c, m
        self.dir = 1 - 2 * c
        self.sent = []

    def rows(self, ref, dz, dx, core):
        block = (((self.z + dz + NZ) % NZ) * NX + (self.x + dx) % NX) * 2 + core
        return ref.at[pl.ds(pl.multiple_of(block * T, T), T)]

    def dev(self, dz, dx, core):
        return ((((self.z + dz + NZ) % NZ) * NX + (self.x + dx) % NX) * 2 + core, self.m)

    def send(self, ref, dz, dx, to_z, to_x, recv, send_sem):
        part = self.rows(ref, dz, dx, self.c)
        copy = pltpu.make_async_remote_copy(
            src_ref=part, dst_ref=part, send_sem=send_sem, recv_sem=recv,
            device_id=self.dev(to_z, to_x, self.c), device_id_type=MESH,
        )
        copy.start()
        self.sent.append(copy)

    def a_z(self, dz, dx, way):
        self.send(self.a, dz, dx, way, 0, self.ra.at[(dz - way) % NZ, dx % NX], self.sza.at[dz % NZ, dx % NX, (way + 1) // 2])

    def a_x(self, to_x):
        self.send(self.a, 0, 0, 0, to_x, self.ra.at[0, (-to_x) % NX], self.sxa.at[to_x])

    def b_z(self, dz, way):
        self.send(self.b, dz, 0, way, 0, self.rb.at[(dz - way) % NZ, 0], self.szb.at[dz % NZ, (way + 1) // 2])

    def b_z_far(self):
        self.send(self.b, -3 * self.dir, 0, self.dir, 0, self.rb.at[4, 0], self.szb.at[3, 0])

    def b_x(self, dz, dx, way):
        self.send(self.b, dz, dx, 0, way, self.rb.at[dz % NZ, (dx - way) % NX], self.sxb.at[dz % NZ, dx % NX, (way + 1) // 2])

    def sib(self, which, dz, dx):
        ref, recv, ssem = (self.a, self.ca, self.sca) if which == 0 else (self.b, self.cb, self.scb)
        part = self.rows(ref, dz, dx, self.c)
        copy = pltpu.make_async_remote_copy(
            src_ref=part, dst_ref=part, send_sem=ssem.at[dz % NZ, dx % NX], recv_sem=recv.at[dz % NZ, dx % NX],
            device_id=self.dev(0, 0, 1 - self.c), device_id_type=MESH,
        )
        copy.start()
        self.sent.append(copy)

    def wait(self, which, dz, dx):
        ref, recv = (self.a, self.ra) if which == 0 else (self.b, self.rb)
        part = self.rows(ref, dz, dx, self.c)
        pltpu.make_async_remote_copy(
            src_ref=part, dst_ref=part, send_sem=self.sxa.at[0], recv_sem=recv.at[dz % NZ, dx % NX],
            device_id=self.dev(0, 0, 1 - self.c), device_id_type=MESH,
        ).wait_recv()

    def wait_sib(self, which, dz, dx):
        ref, recv = (self.a, self.ca) if which == 0 else (self.b, self.cb)
        part = self.rows(ref, dz, dx, 1 - self.c)
        pltpu.make_async_remote_copy(
            src_ref=part, dst_ref=part, send_sem=self.sxa.at[0], recv_sem=recv.at[dz % NZ, dx % NX],
            device_id=self.dev(0, 0, 1 - self.c), device_id_type=MESH,
        ).wait_recv()

    def start_a(self):
        for to_x in (1, 3, 2):
            self.a_x(to_x)
        for way in (1, -1):
            self.a_z(0, 0, way)
        self.sib(0, 0, 0)

    def start_b(self):
        for way in (1, -1):
            self.b_z(0, way)
        for way in (1, -1):
            self.b_x(0, 0, way)
        self.sib(1, 0, 0)

    def first(self):
        for dx in (1, 3, 2):
            self.wait(0, 0, dx)
            for way in (1, -1):
                self.a_z(0, dx, way)
            self.sib(0, 0, dx)
            yield

    def round(self, k):
        if k <= 4:
            for dz in DIST[k]:
                self.wait(1, dz, 0)
                if k < 3:
                    self.b_z(dz, -1 if dz > 0 else 1)
                for way in (1, -1):
                    self.b_x(dz, 0, way)
                self.sib(1, dz, 0)
                yield
            if k == 3:
                self.b_z_far()
        if 1 <= k <= 5:
            for dz in DIST[k - 1]:
                for dx in (1, 3):
                    self.wait(1, dz, dx)
                    if dz % 2 == 0 and dx == 3:
                        self.b_x(dz, dx, 1)
                    if dz % 2 == 1 and dx == 1:
                        self.b_x(dz, dx, -1)
                    self.sib(1, dz, dx)
                    yield
        if 2 <= k <= 6:
            for dz in DIST[k - 2]:
                self.wait(1, dz, 2)
                self.sib(1, dz, 2)
                yield
        if k <= 4:
            for dx in (0, 1, 3, 2):
                for dz in DIST[k]:
                    self.wait(0, dz, dx)
                    way = -1 if dz > 0 else 1
                    if k < 3 or (k == 3 and way == (1 if dx % 2 == 0 else -1)):
                        self.a_z(dz, dx, way)
                    self.sib(0, dz, dx)
                    yield

    def finish(self):
        for copy in self.sent:
            copy.wait_send()


def drain(steps):
    for _ in steps:
        pass


def kernel(
    frames, ids_in, gain, wq, wk, wv, bq, bk, bv, freq, out,
    fs, a2a_src, a2a_dst, ids_buf, ids_dense, ids_t, tok, wa, wb, kbuf, vbuf, qs, acc, mx, den,
    sa_s, sa_r, si_s, si_r, sy_s, sy_r, sp_s, sp_r, se,
    *gsems,
):
    s = lax.axis_index("seq")
    m = lax.axis_index("mp")
    z, x, c = s // (NX * 2), (s // 2) % NX, s % 2
    wg = Gather(wa, wb, gsems[:10], z, x, c, m)
    kg = Gather(kbuf, vbuf, gsems[10:], z, x, c, m)
    sent = []

    barrier = pltpu.get_barrier_semaphore()

    @pl.loop(1, NS)
    def _(k):
        pl.semaphore_signal(barrier, inc=1, device_id=((s + k) % NS, m), device_id_type=MESH)

    @pl.loop(1, NM)
    def _(k):
        pl.semaphore_signal(barrier, inc=1, device_id=(s, (m + k) % NM), device_id_type=MESH)

    for j in range(8):
        fs[pl.ds(j, T, stride=8), :] = frames[:, j * 128:(j + 1) * 128].astype(jnp.float32)
    a2a_src[...] = fs[...].astype(jnp.bfloat16)
    own = pl.ds(pl.multiple_of(s * T, T), T)
    head_cols = pl.ds(pl.multiple_of((m // 2) * HD, HD), HD)
    is_key = m % 2 == 0
    wa[own, :] = wq[:, 0:CA]
    wb[own, 0:512 - CA] = wq[:, CA:512]

    @pl.when(is_key)
    def _():
        wb[own, 512 - CA:CB] = wk[:, head_cols]

    @pl.when(jnp.logical_not(is_key))
    def _():
        wb[own, 512 - CA:CB] = wv[:, head_cols]

    def block16(ref, index):
        return ref.at[pl.ds(pl.multiple_of(index * 16, 16), 16)]

    mine16 = pl.ds(pl.multiple_of(s * 16, 16), 16)
    a2a_dst[mine16, :] = a2a_src[mine16, :]
    ids_buf[pl.ds(s, 1)] = ids_in[pl.ds(s, 1)]
    pl.semaphore_wait(barrier, NS - 1 + NM - 1)

    def a2a_copy(dst_dev, src_block, dst_block, k):
        return pltpu.make_async_remote_copy(
            src_ref=block16(a2a_src, src_block), dst_ref=block16(a2a_dst, dst_block),
            send_sem=sa_s.at[k], recv_sem=sa_r.at[k], device_id=(dst_dev, m), device_id_type=MESH,
        )

    @pl.loop(1, NS)
    def _(k):
        a2a_copy((s + k) % NS, (s + k) % NS, s, k).start()

    wg.start_b()
    wg.start_a()

    def id_copy(dst_dev, src_block, dst_block, send_k, recv_k):
        return pltpu.make_async_remote_copy(
            src_ref=ids_in.at[src_block], dst_ref=ids_buf.at[dst_block],
            send_sem=si_s.at[send_k], recv_sem=si_r.at[recv_k], device_id=(dst_dev, m), device_id_type=MESH,
        )

    @pl.loop(0, NZ)
    def _(k):
        target = k * 8 + m

        @pl.when(target != s)
        def _():
            id_copy(target, target, s, k, s).start()

    drain(wg.first())

    @pl.loop(1, NS)
    def _(k):
        a2a_copy((s + k) % NS, (s + k) % NS, (s - k + NS) % NS, k).wait_recv()

    fs[...] = a2a_dst[...].astype(jnp.float32)
    for j in range(8):
        tok[m, :, j * 128:(j + 1) * 128] = fs[pl.ds(j, T, stride=8), :].astype(jnp.bfloat16)

    def y_copy(d, half, way):
        part = tok.at[(m + d + NM) % NM, pl.ds(half * 64, 64)]
        return pltpu.make_async_remote_copy(
            src_ref=part, dst_ref=part, send_sem=sy_s.at[d % NM, half, (way + 1) // 2],
            recv_sem=sy_r.at[(d - way) % NM, half], device_id=(s, (m + way + NM) % NM), device_id_type=MESH,
        )

    def y_send(d, half, way):
        copy = y_copy(d, half, way)
        copy.start()
        sent.append(copy)

    def y_wait(d, half):
        part = tok.at[(m + d + NM) % NM, pl.ds(half * 64, 64)]
        pltpu.make_async_remote_copy(
            src_ref=part, dst_ref=part, send_sem=sy_s.at[0, 0, 0], recv_sem=sy_r.at[d % NM, half],
            device_id=(s, (m + 1) % NM), device_id_type=MESH,
        ).wait_recv()

    for half in (0, 1):
        for way in (1, -1):
            y_send(0, half, way)

    def y_steps():
        for k in (1, 2, 3, 4):
            for half in (0, 1):
                for d in DIST[k]:
                    y_wait(d, half)
                    way = -1 if d > 0 else 1
                    if k < 3 or (k == 3 and way == (1 if half == 0 else -1)):
                        y_send(d, half, way)
                    yield

    def p_copy(way_k, recv_k):
        return pltpu.make_async_remote_copy(
            src_ref=ids_t, dst_ref=ids_t, send_sem=sp_s.at[way_k], recv_sem=sp_r.at[recv_k],
            device_id=(s, (m + way_k) % NM), device_id_type=MESH,
        )

    collector = s % NM == m

    @pl.when(collector)
    def _():
        @pl.loop(0, NS)
        def _(src):
            @pl.when(src != s)
            def _():
                id_copy((s + 1) % NS, 0, src, 0, src).wait_recv()

        for src in range(NS):
            ids_dense[2 * src:2 * src + 2, :] = ids_buf[src]
        ids_t[...] = ids_dense[...].T[0:8, :]

        @pl.loop(1, NM)
        def _(k):
            p_copy(k, 0).start()

    yield_y = y_steps()
    count = 0
    for k in range(1, 7):
        for _ in wg.round(k):
            count += 1
            if count % 3 == 0:
                next(yield_y, None)
    drain(yield_y)

    @pl.when(jnp.logical_not(collector))
    def _():
        p_copy(1, 0).wait_recv()

    lane = lax.broadcasted_iota(jnp.int32, (T, HD), 1) % (HD // 2)
    columns = jnp.concatenate([ids_t[...], jnp.zeros((HD - 8, T), jnp.float32)], axis=0).T
    chosen = jnp.where(lane < 16, columns[:, 0:1], jnp.where(lane < 40, columns[:, 1:2], columns[:, 2:3]))
    angle = chosen * freq[...]
    cosine = jnp.cos(angle)
    sines = jnp.sin(angle)
    signed = jnp.where(lax.broadcasted_iota(jnp.int32, (T, HD), 1) < HD // 2, -sines, sines)

    squares = jnp.zeros((T, 1), jnp.float32)
    for b in range(NM):
        block = tok[b].astype(jnp.float32)
        squares = squares + jnp.sum(block * block, axis=1, keepdims=True)
    inverse = lax.rsqrt(squares / (NM * 1024.0) + 1e-06)
    for dz in range(NZ):
        for dx in range(NX):
            wg.wait_sib(0, dz, dx)
            wg.wait_sib(1, dz, dx)

    def project(b, carry):
        qa, qb = carry
        at = pl.ds(pl.multiple_of(b * 1024, 1024), 1024)
        normed = (tok[b].astype(jnp.float32) * inverse * gain[:, at].astype(jnp.float32)).astype(jnp.bfloat16)
        qa = qa + jnp.dot(normed, wa[at, :], preferred_element_type=jnp.float32)
        qb = qb + jnp.dot(normed, wb[at, :], preferred_element_type=jnp.float32)
        return qa, qb

    qa, qb = lax.fori_loop(
        0, NM, project, (jnp.zeros((T, CA), jnp.float32), jnp.zeros((T, CB), jnp.float32))
    )

    def rotate(part):
        return (part * cosine + pltpu.roll(part, HD // 2, axis=1) * signed).astype(jnp.bfloat16)

    kv = qb[:, 512 - CA:CB]

    def exchange(ref):
        part = ref.at[own]
        return pltpu.make_async_remote_copy(
            src_ref=part, dst_ref=part, send_sem=se.at[0], recv_sem=se.at[1],
            device_id=(s, m + 1 - 2 * (m % 2)), device_id_type=MESH,
        )

    @pl.when(is_key)
    def _():
        kbuf[own, :] = rotate(kv + bk[:, head_cols].astype(jnp.float32))
        exchange(kbuf).start()

    @pl.when(jnp.logical_not(is_key))
    def _():
        vbuf[own, :] = (kv + bv[:, head_cols].astype(jnp.float32)).astype(jnp.bfloat16)
        exchange(vbuf).start()

    for h in range(4):
        part = qa[:, h * HD:(h + 1) * HD] if h * HD < CA else qb[:, h * HD - CA:(h + 1) * HD - CA]
        qs[h] = rotate(part + bq[:, h * HD:(h + 1) * HD].astype(jnp.float32))
    acc[...] = jnp.zeros_like(acc)
    den[...] = jnp.zeros_like(den)
    mx[...] = jnp.full(mx.shape, -1e30, jnp.float32)

    exchange(kbuf).wait_recv()
    exchange(kbuf).wait_send()
    kg.start_a()
    kg.start_b()

    def slab_body(first_row, masked):
        at = pl.ds(pl.multiple_of(first_row, 1024), 1024)

        @pl.loop(0, 4)
        def _(h):
            scores = lax.dot_general(
                qs[h], kbuf[at, :], (((1,), (1,)), ((), ())), preferred_element_type=jnp.float32
            )
            if masked:
                row = lax.broadcasted_iota(jnp.int32, scores.shape, 0) + (x * 2 + c) * T
                visible = lax.broadcasted_iota(jnp.int32, scores.shape, 1) <= row
                scores = jnp.where(visible, scores, -1e30)
            old = mx[h][:, 0:1]
            new = jnp.maximum(old, jnp.max(scores, axis=1, keepdims=True))
            factor = jnp.exp2((old - new) * EXP_SCALE)
            terms = jnp.exp2((scores - new) * EXP_SCALE)
            if masked:
                terms = jnp.where(visible, terms, 0.0)
            total = den[h][:, 0:1] * factor + jnp.sum(terms, axis=1, keepdims=True)
            acc[h] = acc[h] * factor + jnp.dot(
                terms.astype(jnp.bfloat16), vbuf[at, :], preferred_element_type=jnp.float32
            )
            mx[h] = jnp.broadcast_to(new, (T, HD))
            den[h] = jnp.broadcast_to(total, (T, HD))

    def slab(dz):
        for dx in range(NX):
            kg.wait_sib(0, dz, dx)
            kg.wait_sib(1, dz, dx)
        if dz == 0:
            slab_body(z * 1024, True)
        else:
            zz = (z + dz + NZ) % NZ

            @pl.when(zz < z)
            def _():
                slab_body(zz * 1024, False)

    drain(kg.first())
    for k in range(1, 7):
        drain(kg.round(k))
        if k >= 2:
            for dz in DIST[k - 2]:
                slab(dz)

    for h in range(4):
        out[:, h * HD:(h + 1) * HD] = (acc[h] / den[h]).astype(jnp.bfloat16)

    @pl.loop(1, NS)
    def _(k):
        a2a_copy((s + k) % NS, (s + k) % NS, s, k).wait_send()

    @pl.loop(0, NZ)
    def _(k):
        target = k * 8 + m

        @pl.when(target != s)
        def _():
            id_copy(target, target, s, k, s).wait_send()

    @pl.when(collector)
    def _():
        @pl.loop(1, NM)
        def _(k):
            p_copy(k, 0).wait_send()

    for copy in sent:
        copy.wait_send()
    wg.finish()
    kg.finish()


def gather_sems():
    dma = pltpu.SemaphoreType.DMA
    return [
        dma((NZ, NX)), dma((NZ, NX)), dma((NZ, NX)), dma((NZ, NX)),
        dma((NZ, NX, 2)), dma((NX,)), dma((NZ, 2)), dma((NZ, NX, 2)), dma((NZ, NX)), dma((NZ, NX)),
    ]


def shards(frames_tokens, positions, norm_gain, w_query, w_key, w_value, b_query, b_key, b_value):
    dma = pltpu.SemaphoreType.DMA
    ids = jnp.pad(positions.astype(jnp.float32).reshape(NS, 2, 3), ((0, 0), (0, 0), (0, HD - 3)))
    half = np.power(1000000.0, -(2.0 * np.arange(HD // 2)) / HD).astype(np.float32)
    freq = jnp.asarray(np.concatenate([half, half])[None, :])
    vmem = pl.BlockSpec(memory_space=pltpu.VMEM)
    return pl.pallas_call(
        kernel,
        name="fused",
        out_shape=jax.ShapeDtypeStruct((T, 512), jnp.bfloat16),
        in_specs=[vmem] * 10,
        out_specs=vmem,
        scratch_shapes=[
            pltpu.VMEM((1024, 128), jnp.float32),
            pltpu.VMEM((1024, 128), jnp.bfloat16),
            pltpu.VMEM((1024, 128), jnp.bfloat16),
            pltpu.VMEM((NS, 2, HD), jnp.float32),
            pltpu.VMEM((T, HD), jnp.float32),
            pltpu.VMEM((8, T), jnp.float32),
            pltpu.VMEM((NM, T, 1024), jnp.bfloat16),
            pltpu.VMEM((NS * T, CA), jnp.bfloat16),
            pltpu.VMEM((NS * T, CB), jnp.bfloat16),
            pltpu.VMEM((NS * T, HD), jnp.bfloat16),
            pltpu.VMEM((NS * T, HD), jnp.bfloat16),
            pltpu.VMEM((4, T, HD), jnp.bfloat16),
            pltpu.VMEM((4, T, HD), jnp.float32),
            pltpu.VMEM((4, T, HD), jnp.float32),
            pltpu.VMEM((4, T, HD), jnp.float32),
            dma((NS,)), dma((NS,)), dma((NZ,)), dma((NS,)),
            dma((NM, 2, 2)), dma((NM, 2)), dma((NM,)), dma((1,)), dma((2,)),
        ] + gather_sems() + gather_sems(),
        compiler_params=pltpu.CompilerParams(
            collective_id=0, has_side_effects=True, vmem_limit_bytes=52 * 2**20
        ),
        cost_estimate=pl.CostEstimate(flops=5 * 10**9, bytes_accessed=10**7, transcendentals=4 * 10**6),
    )(
        frames_tokens, ids, norm_gain[None, :], w_query, w_key, w_value,
        b_query[None, :], b_key[None, :], b_value[None, :], freq,
    )


def solution(mesh):
    in_specs = (
        P("seq", "mp"), P("seq", None), P(), P("seq", "mp"), P("seq", None), P("seq", None),
        P("mp"), P(), P(),
    )
    return jax.shard_map(shards, mesh=mesh, in_specs=in_specs, out_specs=P("seq", "mp"), check_vma=False)
```

time: 546 us -> 113 us (0.21)
  the two profiles are of different devices: /device:TPU:449 before, /device:TPU:457 now
where the time goes in v1:
time: 113 us
  Pallas kernels  105 us (93%)
  local copies, waits for them, and re-layouts  6.9 us (6%)
    pallas_call x1, Pallas kernels, shards(): pl.pallas_call(kernel, name='fused', out_shape=jax.ShapeDtypeStruct((T, 5...  105 us
    unnamed x11, local copies, waits for them, and re-layouts  3.98 us

profile of v1, /device:TPU:457, one launch (start us, length us, event | category | flops | bytes accessed | tf_op | source)
XLA Modules:
  0.0 112.8 jit_solution(12682822271702763627)
XLA Ops:
  0.0 0.0 copy-start
  0.0 0.7 convert_element_type.5
  0.7 0.7 broadcast_in_dim.13.bq
  1.4 0.7 broadcast_in_dim.14.bk
  2.1 0.7 broadcast_in_dim.15.bv
  2.8 0.7 broadcast_in_dim.12.gain
  3.5 0.1 copy.11
  3.6 0.0 copy-start.4
  3.7 0.0 copy-done
  3.7 0.6 copy-done.4
  4.3 0.0 copy-start.1
  4.3 0.9 copy-done.1
  5.2 0.0 copy-start.2
  5.2 0.9 copy-done.2
  6.1 0.0 copy-start.3
  6.1 0.9 copy-done.3
  7.0 105.1 %fused.1 = bf16[128,512]{1,0:T(8,128)(2,1)S(1)} custom-call(bf16[128,1024]{1,0:T(8,128)(2,1)S(1)} %copy-done, f32[64,2,128]{2,1,0:T(2,128)S(1)} %pad.4.ids_in, bf16[1,8192]{1,0:T(2,128)(2,1)S(1)} %broadcast_in_dim.12.gain, bf16[128,512]{1,0:T(8,128)(2,1)S(1)} %copy-done.1, bf16[128,512]{1,0:T(8,128)(2,1)S(1)} %copy-done.2, bf16[128,512]{1,0:T(8,128)(2,1)S(1)} %copy-done.3, ...), custom_call_target="tpu_custom_call" | custom-call | flops 5000000000 | bytes 10000000 | tf_op jit(solution)/shard_map/fused/pallas_call | solution.py:461
  112.1 0.7 copy.13
  (1 shorter events, 0.0 us)
Async XLA Ops:
  0.0 3.7 %copy-start = (bf16[128,1024]{1,0:T(8,128)(2,1)S(1)}, bf16[128,1024]{1,0:T(8,128)(2,1)}, u32[]{:S(2)}) copy-start(bf16[128,1024]{1,0:T(8,128)(2,1)} %frames.1) | copy-start | bytes 786436
  3.6 0.7 copy-start.4
  4.3 0.9 copy-start.1
  5.2 0.9 copy-start.2
  6.1 0.9 copy-start.3

commit v2 on v1

v2 whole, which is shorter than its diff:
```python
import functools
import math

import jax
import jax.numpy as jnp
import numpy as np
from jax import lax
from jax.experimental import pallas as pl
from jax.experimental.pallas import tpu as pltpu
from jax.sharding import PartitionSpec as P

HD = 128
T = 128
NX, NZ, NM = 4, 8, 8
NS = NZ * NX * 2
CA, CB = 256, 384
MESH = pl.DeviceIdType.MESH
DIST = [[0], [-1, 1], [-2, 2], [-3, 3], [4]]
EXP_SCALE = math.log2(math.e) / math.sqrt(HD)


class Gather:
    def __init__(self, a, b, sems, z, x, c, m, direct_b):
        self.a, self.b = a, b
        self.ra, self.rb, self.ca, self.cb, self.sa, self.sb = sems
        self.z, self.x, self.c, self.m = z, x, c, m
        self.dir = 1 - 2 * c
        self.direct_b = direct_b

    def rows(self, ref, dz, dx, core):
        block = (core * NZ + (self.z + dz + NZ) % NZ) * NX + (self.x + dx) % NX
        return ref.at[pl.ds(pl.multiple_of(block * T, T), T)]

    def four(self, ref, dz, core):
        first = (core * NZ + (self.z + dz + NZ) % NZ) * NX
        return ref.at[pl.ds(pl.multiple_of(first * T, NX * T), NX * T)]

    def dev(self, dz, dx, core):
        return ((((self.z + dz + NZ) % NZ) * NX + (self.x + dx) % NX) * 2 + core, self.m)

    def copy(self, part, send_sem, recv_sem, device):
        return pltpu.make_async_remote_copy(
            src_ref=part, dst_ref=part, send_sem=send_sem, recv_sem=recv_sem,
            device_id=device, device_id_type=MESH,
        )

    def send(self, ref, dz, dx, to_z, to_x, recv, send_sem):
        self.copy(self.rows(ref, dz, dx, self.c), send_sem, recv, self.dev(to_z, to_x, self.c)).start()

    def a_z(self, dz, dx, way):
        self.send(self.a, dz, dx, way, 0, self.ra.at[(dz - way) % NZ, dx % NX], self.sa.at[0])

    def a_x(self, to_x):
        self.send(self.a, 0, 0, 0, to_x, self.ra.at[0, (-to_x) % NX], self.sa.at[0])

    def b_z(self, dz, way):
        self.send(self.b, dz, 0, way, 0, self.rb.at[(dz - way) % NZ, 0], self.sb.at[0])

    def b_z_far(self):
        self.send(self.b, -3 * self.dir, 0, self.dir, 0, self.rb.at[4, 0], self.sb.at[0])

    def b_x(self, dz):
        for to_x in (1, 3, 2):
            self.send(self.b, dz, 0, 0, to_x, self.rb.at[dz % NZ, (-to_x) % NX], self.sb.at[0])

    def sib(self, which, dz):
        ref, recv, send = (self.a, self.ca, self.sa) if which == 0 else (self.b, self.cb, self.sb)
        self.copy(self.four(ref, dz, self.c), send.at[1], recv.at[dz % NZ], self.dev(0, 0, 1 - self.c)).start()

    def wait(self, which, dz, dx):
        ref, recv, send = (self.a, self.ra, self.sa) if which == 0 else (self.b, self.rb, self.sb)
        self.copy(
            self.rows(ref, dz, dx, self.c), send.at[0], recv.at[dz % NZ, dx % NX], self.dev(0, 0, 1 - self.c)
        ).wait_recv()

    def wait_sib(self, which, dz):
        ref, recv, send = (self.a, self.ca, self.sa) if which == 0 else (self.b, self.cb, self.sb)
        self.copy(
            self.four(ref, dz, 1 - self.c), send.at[1], recv.at[dz % NZ], self.dev(0, 0, 1 - self.c)
        ).wait_recv()

    def start_a(self):
        for to_x in (1, 3, 2):
            self.a_x(to_x)
        for way in (1, -1):
            self.a_z(0, 0, way)

    def start_b(self):
        for way in (1, -1, 2, -2, 3, -3, 4) if self.direct_b else (1, -1):
            self.b_z(0, way)
        self.b_x(0)

    def first(self):
        for dx in (1, 3, 2):
            self.wait(0, 0, dx)
            for way in (1, -1):
                self.a_z(0, dx, way)
            yield
        self.sib(0, 0)

    def b_arrive(self, k):
        for dz in DIST[k]:
            self.wait(1, dz, 0)
            if k < 3 and not self.direct_b:
                self.b_z(dz, -1 if dz > 0 else 1)
            self.b_x(dz)
            yield
        if k == 3 and not self.direct_b:
            self.b_z_far()

    def b_across(self, k):
        for dz in DIST[k]:
            for dx in (1, 3, 2):
                self.wait(1, dz, dx)
            self.sib(1, dz)
            yield

    def a_arrive(self, k):
        for dx in (0, 1, 3, 2):
            for dz in DIST[k]:
                self.wait(0, dz, dx)
                way = -1 if dz > 0 else 1
                if k < 3 or (k == 3 and way == (1 if dx % 2 == 0 else -1)):
                    self.a_z(dz, dx, way)
                yield
        for dz in DIST[k]:
            self.sib(0, dz)

    def finish(self):
        for ref, send in ((self.a, self.sa), (self.b, self.sb)):
            for k, count in ((0, 31), (1, 32)):
                self.copy(ref.at[pl.ds(0, count * T)], send.at[k], send.at[k], self.dev(0, 0, 1 - self.c)).wait_send()


def drain(steps):
    for _ in steps:
        pass


def kernel(
    frames_in, ids_hbm, gain_hbm, wq, wk, wv, bq_hbm, bk_hbm, bv_hbm, freq_hbm, out,
    frames, ids_in, gain, bq, bk, bv, freq, fs, a2a_src, a2a_dst, ids_src, ids_buf, ids_dense, ids_t, tok, nrm, wa, wb, kv, qs, acc, mx, den,
    squares, tables, biases, s_in, sa_s, sa_r, si_s, si_r, sy_s, sy_r, sp_s, sp_r, se,
    *gsems,
):
    s = lax.axis_index("seq")
    m = lax.axis_index("mp")
    z, x, c = s // (NX * 2), (s // 2) % NX, s % 2
    wg = Gather(wa, wb, gsems[:6], z, x, c, m, False)
    own_kind, other_kind = kv.at[pl.ds(0, NS * T)], kv.at[pl.ds(NS * T, NS * T)]
    kg = Gather(other_kind, own_kind, gsems[6:], z, x, c, m, True)

    barrier = pltpu.get_barrier_semaphore()

    block = (c * NZ + z) * NX + x
    own = pl.ds(pl.multiple_of(block * T, T), T)
    head_cols = pl.ds(pl.multiple_of((m // 2) * HD, HD), HD)
    is_key = m % 2 == 0
    load_frames = pltpu.make_async_copy(frames_in, frames, s_in.at[0])
    load_qa = pltpu.make_async_copy(wq.at[:, pl.ds(0, CA)], wa.at[own], s_in.at[1])
    load_qb = pltpu.make_async_copy(wq.at[:, pl.ds(CA, 512 - CA)], wb.at[own, pl.ds(0, 512 - CA)], s_in.at[2])
    load_k = pltpu.make_async_copy(wk.at[:, head_cols], wb.at[own, pl.ds(512 - CA, HD)], s_in.at[3])
    load_v = pltpu.make_async_copy(wv.at[:, head_cols], wb.at[own, pl.ds(512 - CA, HD)], s_in.at[3])
    small = [
        pltpu.make_async_copy(src, dst, s_in.at[4 + k])
        for k, (src, dst) in enumerate(
            ((ids_hbm, ids_in), (gain_hbm, gain), (bq_hbm, bq), (bk_hbm, bk), (bv_hbm, bv), (freq_hbm, freq))
        )
    ]
    load_frames.start()
    for copy in small:
        copy.start()
    load_qa.start()
    load_qb.start()

    @pl.when(is_key)
    def _():
        load_k.start()

    @pl.when(jnp.logical_not(is_key))
    def _():
        load_v.start()

    @pl.loop(1, NS)
    def _(k):
        pl.semaphore_signal(barrier, inc=1, device_id=((s + k) % NS, m), device_id_type=MESH)

    @pl.loop(1, NM)
    def _(k):
        pl.semaphore_signal(barrier, inc=1, device_id=(s, (m + k) % NM), device_id_type=MESH)

    def block16(ref, index):
        return ref.at[pl.ds(pl.multiple_of(index * 16, 16), 16)]

    mine16 = pl.ds(pl.multiple_of(s * 16, 16), 16)
    load_frames.wait()
    for copy in small:
        copy.wait()
    for j in range(8):
        fs[pl.ds(j, T, stride=8), :] = frames[:, j * 128:(j + 1) * 128].astype(jnp.float32)
    a2a_src[...] = fs[...].astype(jnp.bfloat16)
    a2a_dst[mine16, :] = a2a_src[mine16, :]
    ids_rows = jnp.concatenate([ids_in[...].astype(jnp.float32), jnp.zeros((HD - 3, T), jnp.float32)], axis=0).T
    for k in range(NS):
        ids_src[k] = ids_rows[2 * k:2 * k + 2, :]
    ids_buf[pl.ds(s, 1)] = ids_src[pl.ds(s, 1)]
    for row, ref in enumerate((bq, bk, bv)):
        biases[row:row + 1, :] = ref[...].astype(jnp.float32).reshape(1, 512)
    load_qa.wait()
    load_qb.wait()
    load_k.wait()
    pl.semaphore_wait(barrier, NS - 1 + NM - 1)

    wg.start_b()
    wg.start_a()

    def a2a_copy(dst_dev, src_block, dst_block):
        return pltpu.make_async_remote_copy(
            src_ref=block16(a2a_src, src_block), dst_ref=block16(a2a_dst, dst_block),
            send_sem=sa_s.at[0], recv_sem=sa_r.at[0], device_id=(dst_dev, m), device_id_type=MESH,
        )

    @pl.loop(1, NS)
    def _(k):
        a2a_copy((s + k) % NS, (s + k) % NS, s).start()

    a2a_all = pltpu.make_async_remote_copy(
        src_ref=a2a_src.at[pl.ds(0, (NS - 1) * 16)], dst_ref=a2a_dst.at[pl.ds(0, (NS - 1) * 16)],
        send_sem=sa_s.at[0], recv_sem=sa_r.at[0], device_id=((s + 1) % NS, m), device_id_type=MESH,
    )

    def id_copy(target, k):
        return pltpu.make_async_remote_copy(
            src_ref=ids_src.at[target], dst_ref=ids_buf.at[s],
            send_sem=si_s.at[k], recv_sem=si_r.at[0], device_id=(target, m), device_id_type=MESH,
        )

    @pl.loop(0, NZ)
    def _(k):
        target = k * 8 + m

        @pl.when(target != s)
        def _():
            id_copy(target, k).start()

    drain(wg.first())
    a2a_all.wait_recv()
    fs[...] = a2a_dst[...].astype(jnp.float32)
    for j in range(8):
        tok[m, :, j * 128:(j + 1) * 128] = fs[pl.ds(j, T, stride=8), :].astype(jnp.bfloat16)

    def y_send(d, half, way):
        part = tok.at[(m + d + NM) % NM, pl.ds(half * 64, 64)]
        pltpu.make_async_remote_copy(
            src_ref=part, dst_ref=part, send_sem=sy_s.at[0],
            recv_sem=sy_r.at[(d - way) % NM, half], device_id=(s, (m + way + NM) % NM), device_id_type=MESH,
        ).start()

    def y_wait(d, half):
        part = tok.at[(m + d + NM) % NM, pl.ds(half * 64, 64)]
        pltpu.make_async_remote_copy(
            src_ref=part, dst_ref=part, send_sem=sy_s.at[0], recv_sem=sy_r.at[d % NM, half],
            device_id=(s, (m + 1) % NM), device_id_type=MESH,
        ).wait_recv()

    for half in (0, 1):
        for way in (1, -1):
            y_send(0, half, way)

    squares[...] = jnp.zeros_like(squares)

    def add_squares(d, half):
        rows = pl.ds(half * 64, 64)
        total = squares[rows, :]
        for j in range(8):
            part = tok[(m + d + NM) % NM, rows, j * 128:(j + 1) * 128].astype(jnp.float32)
            total = total + part * part
        squares[rows, :] = total

    for half in (0, 1):
        add_squares(0, half)

    def y_steps():
        for k in (1, 2, 3, 4):
            for half in (0, 1):
                for d in DIST[k]:
                    y_wait(d, half)
                    way = -1 if d > 0 else 1
                    if k < 3 or (k == 3 and way == (1 if half == 0 else -1)):
                        y_send(d, half, way)
                    add_squares(d, half)
                    yield

    def p_copy(way_k):
        return pltpu.make_async_remote_copy(
            src_ref=ids_t, dst_ref=ids_t, send_sem=sp_s.at[way_k],
            recv_sem=sp_r.at[0], device_id=(s, (m + way_k) % NM), device_id_type=MESH,
        )

    collector = s % NM == m

    def collect_ids():
        @pl.when(collector)
        def _():
            pltpu.make_async_remote_copy(
                src_ref=ids_src.at[pl.ds(0, NS - 1)], dst_ref=ids_buf.at[pl.ds(0, NS - 1)],
                send_sem=si_s.at[0], recv_sem=si_r.at[0], device_id=((s + 1) % NS, m), device_id_type=MESH,
            ).wait_recv()
            for src in range(NS):
                ids_dense[2 * src:2 * src + 2, :] = ids_buf[src]
            ids_t[...] = ids_dense[...].T[0:8, :]

            @pl.loop(1, NM)
            def _(k):
                p_copy(k).start()

    def make_tables():
        @pl.when(jnp.logical_not(collector))
        def _():
            p_copy(1).wait_recv()

        lane = lax.broadcasted_iota(jnp.int32, (T, HD), 1)
        front = lane < HD // 2
        place = jnp.where(front, lane, lane - HD // 2)
        columns = jnp.concatenate([ids_t[...], jnp.zeros((HD - 8, T), jnp.float32)], axis=0).T
        chosen = jnp.where(place < 16, columns[:, 0:1], jnp.where(place < 40, columns[:, 1:2], columns[:, 2:3]))
        angle = chosen * freq[...]
        sines = jnp.sin(angle)
        tables[0] = jnp.cos(angle)
        tables[1] = jnp.where(front, -sines, sines)

    def weight_steps():
        yield from wg.b_arrive(1)
        yield from wg.b_across(0)
        yield from wg.a_arrive(1)
        collect_ids()
        yield from wg.b_arrive(2)
        yield from wg.b_across(1)
        yield from wg.a_arrive(2)
        yield from wg.b_arrive(3)
        yield from wg.b_across(2)
        yield from wg.a_arrive(3)
        make_tables()
        yield from wg.b_arrive(4)
        yield from wg.b_across(3)
        yield from wg.a_arrive(4)
        yield from wg.b_across(4)

    ring = y_steps()
    for index, _ in enumerate(weight_steps()):
        if index >= 4 and index % 5 < 2:
            next(ring, None)
    drain(ring)

    inverse = lax.rsqrt(jnp.sum(squares[...], axis=1, keepdims=True) / (NM * 1024.0) + 1e-06)
    acc[...] = jnp.zeros_like(acc)
    den[...] = jnp.zeros_like(den)
    mx[...] = jnp.full(mx.shape, -1e30, jnp.float32)
    for dz in range(NZ):
        wg.wait_sib(0, dz)
        wg.wait_sib(1, dz)

    def of_core(block, core):
        cols = [block[:, (k * 2 + core) * T:(k * 2 + core + 1) * T] for k in range(NX)]
        return jnp.concatenate(cols, axis=1)

    def core_rows(b, core):
        return pl.ds(pl.multiple_of((core * NZ + b) * NX * T, NX * T), NX * T)

    def project_kv(b, total):
        at = pl.ds(pl.multiple_of(b * 1024, 1024), 1024)
        scale = gain[at].astype(jnp.float32).reshape(1, 1024)
        normed = (tok[b].astype(jnp.float32) * inverse * scale).astype(jnp.bfloat16)
        nrm[b] = normed
        for core in (0, 1):
            total = total + jnp.dot(
                of_core(normed, core), wb[core_rows(b, core), 512 - CA:CB], preferred_element_type=jnp.float32
            )
        return total

    linear = lax.fori_loop(0, NM, project_kv, jnp.zeros((T, HD), jnp.float32))

    def rotate(part):
        return part * tables[0] + pltpu.roll(part, HD // 2, axis=1) * tables[1]

    linear = linear + jnp.where(is_key, biases[1:2, head_cols], biases[2:3, head_cols])
    own_kind[own, :] = jnp.where(is_key, rotate(linear), linear).astype(jnp.bfloat16)

    exchange = pltpu.make_async_remote_copy(
        src_ref=own_kind.at[own], dst_ref=other_kind.at[own], send_sem=se.at[0], recv_sem=se.at[1],
        device_id=(s, m + 1 - 2 * (m % 2)), device_id_type=MESH,
    )
    exchange.start()
    kg.start_b()

    def project_q(b, carry):
        qa, qb = carry
        for core in (0, 1):
            rows = core_rows(b, core)
            part = of_core(nrm[b], core)
            qa = qa + jnp.dot(part, wa[rows, :], preferred_element_type=jnp.float32)
            qb = qb + jnp.dot(part, wb[rows, 0:512 - CA], preferred_element_type=jnp.float32)
        return qa, qb

    zeros = jnp.zeros((T, CA), jnp.float32)
    qa, qb = lax.fori_loop(0, NM, project_q, (zeros, zeros))
    exchange.wait_recv()
    kg.start_a()

    for h in range(4):
        part = (qa, qb)[h // 2][:, (h % 2) * HD:(h % 2 + 1) * HD]
        qs[h] = rotate(part + biases[0:1, h * HD:(h + 1) * HD]).astype(jnp.bfloat16)

    key_base = jnp.where(is_key, 0, NS * T)

    def slab_body(zz, masked):
        def rows_of(base, core):
            return pl.ds(pl.multiple_of(base + (core * NZ + zz) * NX * T, NX * T), NX * T)

        @pl.loop(0, 4)
        def _(h):
            scores = jnp.concatenate(
                [
                    lax.dot_general(
                        qs[h], kv[rows_of(key_base, core), :], (((1,), (1,)), ((), ())),
                        preferred_element_type=jnp.float32,
                    )
                    for core in (0, 1)
                ],
                axis=1,
            )
            if masked:
                row = lax.broadcasted_iota(jnp.int32, scores.shape, 0) + (x * 2 + c) * T
                lane = lax.broadcasted_iota(jnp.int32, scores.shape, 1)
                blk = lane // T
                key = jnp.where(blk < NX, blk * 2, (blk - NX) * 2 + 1) * T + (lane - blk * T)
                visible = key <= row
                scores = jnp.where(visible, scores, -1e30)
            old = mx[h][:, 0:1]
            new = jnp.maximum(old, jnp.max(scores, axis=1, keepdims=True))
            factor = jnp.exp2((old - new) * EXP_SCALE)
            terms = jnp.exp2((scores - new) * EXP_SCALE)
            if masked:
                terms = jnp.where(visible, terms, 0.0)
            total = den[h][:, 0:1] * factor + jnp.sum(terms, axis=1, keepdims=True)
            probs = terms.astype(jnp.bfloat16)
            mixed = acc[h] * factor
            for core in (0, 1):
                mixed = mixed + jnp.dot(
                    probs[:, core * NX * T:(core + 1) * NX * T], kv[rows_of(NS * T - key_base, core), :],
                    preferred_element_type=jnp.float32,
                )
            acc[h] = mixed
            mx[h] = jnp.broadcast_to(new, (T, HD))
            den[h] = jnp.broadcast_to(total, (T, HD))

    def slab(k):
        for dz in DIST[k]:
            kg.wait_sib(0, dz)
            kg.wait_sib(1, dz)
            if dz == 0:
                slab_body(z, True)
            else:
                zz = (z + dz + NZ) % NZ

                @pl.when(zz < z)
                def _():
                    slab_body(zz, False)

    drain(kg.b_arrive(1))
    drain(kg.first())
    drain(kg.b_arrive(2))
    drain(kg.b_across(0))
    drain(kg.b_arrive(3))
    drain(kg.a_arrive(1))
    drain(kg.b_arrive(4))
    drain(kg.b_across(1))
    slab(0)
    drain(kg.a_arrive(2))
    drain(kg.b_across(2))
    slab(1)
    drain(kg.a_arrive(3))
    drain(kg.b_across(3))
    slab(2)
    drain(kg.a_arrive(4))
    drain(kg.b_across(4))
    slab(3)
    slab(4)

    for h in range(4):
        out[:, h * HD:(h + 1) * HD] = (acc[h] / den[h]).astype(jnp.bfloat16)

    a2a_all.wait_send()

    @pl.loop(0, NZ)
    def _(k):
        target = k * 8 + m

        @pl.when(target != s)
        def _():
            id_copy(target, k).wait_send()

    @pl.when(collector)
    def _():
        @pl.loop(1, NM)
        def _(k):
            p_copy(k).wait_send()

    exchange.wait_send()
    seven = tok.at[pl.ds(0, 7)]
    pltpu.make_async_remote_copy(
        src_ref=seven, dst_ref=seven, send_sem=sy_s.at[0], recv_sem=sy_r.at[0, 0],
        device_id=(s, (m + 1) % NM), device_id_type=MESH,
    ).wait_send()
    wg.finish()
    kg.finish()


def gather_sems():
    dma = pltpu.SemaphoreType.DMA
    return [dma((NZ, NX)), dma((NZ, NX)), dma((NZ,)), dma((NZ,)), dma((2,)), dma((2,))]


def shards(frames_tokens, positions, norm_gain, w_query, w_key, w_value, b_query, b_key, b_value):
    dma = pltpu.SemaphoreType.DMA
    half = np.power(1000000.0, -(2.0 * np.arange(HD // 2)) / HD).astype(np.float32)
    freq = jnp.asarray(np.concatenate([half, half])[None, :])
    vmem = pl.BlockSpec(memory_space=pltpu.VMEM)
    hbm = pl.BlockSpec(memory_space=pltpu.HBM)
    return pl.pallas_call(
        kernel,
        name="fused",
        out_shape=jax.ShapeDtypeStruct((T, 512), jnp.bfloat16),
        in_specs=[hbm] * 10,
        out_specs=vmem,
        scratch_shapes=[
            pltpu.VMEM((T, 1024), jnp.bfloat16),
            pltpu.VMEM((3, T), jnp.int32),
            pltpu.VMEM((NS * T,), jnp.bfloat16),
            pltpu.VMEM((512,), jnp.bfloat16),
            pltpu.VMEM((512,), jnp.bfloat16),
            pltpu.VMEM((512,), jnp.bfloat16),
            pltpu.VMEM((1, HD), jnp.float32),
            pltpu.VMEM((1024, 128), jnp.float32),
            pltpu.VMEM((1024, 128), jnp.bfloat16),
            pltpu.VMEM((1024, 128), jnp.bfloat16),
            pltpu.VMEM((NS, 2, HD), jnp.float32),
            pltpu.VMEM((NS, 2, HD), jnp.float32),
            pltpu.VMEM((T, HD), jnp.float32),
            pltpu.VMEM((8, T), jnp.float32),
            pltpu.VMEM((NM, T, 1024), jnp.bfloat16),
            pltpu.VMEM((NM, T, 1024), jnp.bfloat16),
            pltpu.VMEM((NS * T, CA), jnp.bfloat16),
            pltpu.VMEM((NS * T, CB), jnp.bfloat16),
            pltpu.VMEM((2 * NS * T, HD), jnp.bfloat16),
            pltpu.VMEM((4, T, HD), jnp.bfloat16),
            pltpu.VMEM((4, T, HD), jnp.float32),
            pltpu.VMEM((4, T, HD), jnp.float32),
            pltpu.VMEM((4, T, HD), jnp.float32),
            pltpu.VMEM((T, HD), jnp.float32),
            pltpu.VMEM((2, T, HD), jnp.float32),
            pltpu.VMEM((8, 512), jnp.float32),
            dma((10,)), dma((1,)), dma((1,)), dma((NZ,)), dma((1,)),
            dma((1,)), dma((NM, 2)), dma((NM,)), dma((1,)), dma((2,)),
        ] + gather_sems() + gather_sems(),
        compiler_params=pltpu.CompilerParams(
            collective_id=0, has_side_effects=True, vmem_limit_bytes=64 * 2**20 - 2**17
        ),
        cost_estimate=pl.CostEstimate(flops=5 * 10**9, bytes_accessed=10**7, transcendentals=4 * 10**6),
    )(
        frames_tokens, positions.T, norm_gain, w_query, w_key, w_value, b_query, b_key, b_value, freq,
    )


def solution(mesh):
    in_specs = (
        P("seq", "mp"), P("seq", None), P(), P("seq", "mp"), P("seq", None), P("seq", None),
        P("mp"), P(), P(),
    )
    return jax.shard_map(shards, mesh=mesh, in_specs=in_specs, out_specs=P("seq", "mp"), check_vma=False)
```

time: 113 us -> 94.7 us (0.84)
  the two profiles are of different devices: /device:TPU:457 before, /device:TPU:1 now
where the time goes in v2:
time: 94.7 us; the launch traced here: 94.6 us
  Pallas kernels  93 us (98%)
  local copies, waits for them, and re-layouts  1.57 us (2%)
    pallas_call x1, Pallas kernels, shards(): pl.pallas_call(kernel, name='fused', out_shape=jax.ShapeDtypeStruct((T, 5...  93 us

profile of v2, /device:TPU:1, one launch (start us, length us, event | category | flops | bytes accessed | tf_op | source)
XLA Modules:
  0.0 94.6 jit_solution(5905273530150102813)
XLA Ops:
  0.0 93.0 %fused.1 = bf16[128,512]{1,0:T(8,128)(2,1)} custom-call(bf16[128,1024]{1,0:T(8,128)(2,1)} %frames_in.1, s32[3,128]{1,0:T(4,128)} %bitcast.1, bf16[8192]{0:T(1024)(128)(2,1)} %gain_hbm.1, bf16[128,512]{1,0:T(8,128)(2,1)} %wq.1, bf16[128,512]{1,0:T(8,128)(2,1)} %wk.1, bf16[128,512]{1,0:T(8,128)(2,1)} %wv.1, bf16[512]{0:T(512)(128)(2,1)} %bq_hbm.1, ...), custom_call_target="tpu_custom_call" | custom-call | flops 5000000000 | bytes 10000000 | tf_op jit(solution)/shard_map/fused/pallas_call | solution.py:530
  93.0 1.6 %copy.12 = bf16[128,512]{1,0:T(8,128)(2,1)} copy(bf16[128,512]{1,0:T(8,128)(2,1)} %fused.1) | data formatting | bytes 262144

commit v3 on v2

--- a/solution.py
+++ b/solution.py
@@ -26,17 +26,22 @@
         self.z, self.x, self.c, self.m = z, x, c, m
         self.dir = 1 - 2 * c
         self.direct_b = direct_b
+        self.zs = [lax.rem(z + dz, NZ) for dz in range(NZ)]
+        self.xs = [lax.rem(x + dx, NX) for dx in range(NX)]
 
     def rows(self, ref, dz, dx, core):
-        block = (core * NZ + (self.z + dz + NZ) % NZ) * NX + (self.x + dx) % NX
+        block = (core * NZ + self.at_z(dz)) * NX + self.xs[dx % NX]
         return ref.at[pl.ds(pl.multiple_of(block * T, T), T)]
 
     def four(self, ref, dz, core):
-        first = (core * NZ + (self.z + dz + NZ) % NZ) * NX
+        first = (core * NZ + self.at_z(dz)) * NX
         return ref.at[pl.ds(pl.multiple_of(first * T, NX * T), NX * T)]
 
     def dev(self, dz, dx, core):
-        return ((((self.z + dz + NZ) % NZ) * NX + (self.x + dx) % NX) * 2 + core, self.m)
+        return ((self.at_z(dz) * NX + self.xs[dx % NX]) * 2 + core, self.m)
+
+    def at_z(self, dz):
+        return self.zs[dz % NZ] if isinstance(dz, int) else lax.rem(self.z + dz + NZ, NZ)
 
     def copy(self, part, send_sem, recv_sem, device):
         return pltpu.make_async_remote_copy(
@@ -57,10 +62,13 @@
         self.send(self.b, dz, 0, way, 0, self.rb.at[(dz - way) % NZ, 0], self.sb.at[0])
 
     def b_z_far(self):
-        self.send(self.b, -3 * self.dir, 0, self.dir, 0, self.rb.at[4, 0], self.sb.at[0])
+        self.send(self.b, -2 * self.dir, 0, 2 * self.dir, 0, self.rb.at[4, 0], self.sb.at[0])
+
+    def straight(self, dz):
+        return self.direct_b or dz == 4
 
     def b_x(self, dz):
-        for to_x in (1, 3, 2):
+        for to_x in (1, 3, 2) if self.straight(dz) else (1, 3):
             self.send(self.b, dz, 0, 0, to_x, self.rb.at[dz % NZ, (-to_x) % NX], self.sb.at[0])
 
     def sib(self, which, dz):
@@ -86,7 +94,7 @@
             self.a_z(0, 0, way)
 
     def start_b(self):
-        for way in (1, -1, 2, -2, 3, -3, 4) if self.direct_b else (1, -1):
+        for way in (1, -1, 2, -2, 3, -3, 4) if self.direct_b else (1, -1, 2, -2):
             self.b_z(0, way)
         self.b_x(0)
 
@@ -101,17 +109,25 @@
     def b_arrive(self, k):
         for dz in DIST[k]:
             self.wait(1, dz, 0)
-            if k < 3 and not self.direct_b:
+            if k == 2 and not self.direct_b:
                 self.b_z(dz, -1 if dz > 0 else 1)
             self.b_x(dz)
             yield
-        if k == 3 and not self.direct_b:
+        if k == 2 and not self.direct_b:
             self.b_z_far()
 
     def b_across(self, k):
         for dz in DIST[k]:
-            for dx in (1, 3, 2):
+            for dx in (1, 3):
                 self.wait(1, dz, dx)
+                if not self.straight(dz) and dx == (3 if dz % 2 == 0 else 1):
+                    way = 1 if dx == 3 else -1
+                    self.send(self.b, dz, dx, 0, way, self.rb.at[dz % NZ, 2], self.sb.at[0])
+                yield
+
+    def b_last(self, k):
+        for dz in DIST[k]:
+            self.wait(1, dz, 2)
             self.sib(1, dz)
             yield
 
@@ -140,7 +156,7 @@
 def kernel(
     frames_in, ids_hbm, gain_hbm, wq, wk, wv, bq_hbm, bk_hbm, bv_hbm, freq_hbm, out,
     frames, ids_in, gain, bq, bk, bv, freq, fs, a2a_src, a2a_dst, ids_src, ids_buf, ids_dense, ids_t, tok, nrm, wa, wb, kv, qs, acc, mx, den,
-    squares, tables, biases, s_in, sa_s, sa_r, si_s, si_r, sy_s, sy_r, sp_s, sp_r, se,
+    line_a, line_b, inverse, sums_src, sums, tables, biases, s_in, sq_s, sq_r, sa_s, sa_r, si_s, si_r, sy_s, sy_r, sp_s, sp_r, se,
     *gsems,
 ):
     s = lax.axis_index("seq")
@@ -183,11 +199,11 @@
 
     @pl.loop(1, NS)
     def _(k):
-        pl.semaphore_signal(barrier, inc=1, device_id=((s + k) % NS, m), device_id_type=MESH)
+        pl.semaphore_signal(barrier, inc=1, device_id=(lax.rem(s + k, NS), m), device_id_type=MESH)
 
     @pl.loop(1, NM)
     def _(k):
-        pl.semaphore_signal(barrier, inc=1, device_id=(s, (m + k) % NM), device_id_type=MESH)
+        pl.semaphore_signal(barrier, inc=1, device_id=(s, lax.rem(m + k, NM)), device_id_type=MESH)
 
     def block16(ref, index):
         return ref.at[pl.ds(pl.multiple_of(index * 16, 16), 16)]
@@ -211,9 +227,6 @@
     load_k.wait()
     pl.semaphore_wait(barrier, NS - 1 + NM - 1)
 
-    wg.start_b()
-    wg.start_a()
-
     def a2a_copy(dst_dev, src_block, dst_block):
         return pltpu.make_async_remote_copy(
             src_ref=block16(a2a_src, src_block), dst_ref=block16(a2a_dst, dst_block),
@@ -222,7 +235,7 @@
 
     @pl.loop(1, NS)
     def _(k):
-        a2a_copy((s + k) % NS, (s + k) % NS, s).start()
+        a2a_copy(lax.rem(s + k, NS), lax.rem(s + k, NS), s).start()
 
     a2a_all = pltpu.make_async_remote_copy(
         src_ref=a2a_src.at[pl.ds(0, (NS - 1) * 16)], dst_ref=a2a_dst.at[pl.ds(0, (NS - 1) * 16)],
@@ -243,6 +256,9 @@
         def _():
             id_copy(target, k).start()
 
+    wg.start_b()
+    wg.start_a()
+    drain(wg.b_arrive(1))
     drain(wg.first())
     a2a_all.wait_recv()
     fs[...] = a2a_dst[...].astype(jnp.float32)
@@ -263,24 +279,54 @@
             device_id=(s, (m + 1) % NM), device_id_type=MESH,
         ).wait_recv()
 
+    line_a[...] = jnp.zeros_like(line_a)
+    line_b[...] = jnp.zeros_like(line_b)
+    acc[...] = jnp.zeros_like(acc)
+    den[...] = jnp.zeros_like(den)
+    mx[...] = jnp.full(mx.shape, -1e30, jnp.float32)
+    squares = jnp.zeros((T, HD), jnp.float32)
+    for j in range(8):
+        part = tok[m, :, j * 128:(j + 1) * 128].astype(jnp.float32)
+        squares = squares + part * part
+    sums_src[...] = jnp.broadcast_to(jnp.sum(squares.T, axis=0, keepdims=True), (8, T))
+    sums[pl.ds(m, 1)] = sums_src[...][None]
+
+    def sums_copy(way_k):
+        return pltpu.make_async_remote_copy(
+            src_ref=sums_src, dst_ref=sums.at[m], send_sem=sq_s.at[way_k], recv_sem=sq_r.at[0],
+            device_id=(s, (m + way_k) % NM), device_id_type=MESH,
+        )
+
+    @pl.loop(1, NM)
+    def _(k):
+        sums_copy(k).start()
+
     for half in (0, 1):
         for way in (1, -1):
             y_send(0, half, way)
 
-    squares[...] = jnp.zeros_like(squares)
-
-    def add_squares(d, half):
+    def find_inverse():
+        pltpu.make_async_remote_copy(
+            src_ref=sums.at[pl.ds(0, NM - 1)], dst_ref=sums.at[pl.ds(0, NM - 1)], send_sem=sq_s.at[0],
+            recv_sem=sq_r.at[0], device_id=(s, (m + 1) % NM), device_id_type=MESH,
+        ).wait_recv()
+        total = sums[0]
+        for k in range(1, NM):
+            total = total + sums[k]
+        row = lax.rsqrt(total[0:1, :] / (NM * 1024.0) + 1e-06)
+        inverse[...] = jnp.broadcast_to(row, (T, T)).T
+
+    def normalise(d, half):
+        b = (m + d + NM) % NM
         rows = pl.ds(half * 64, 64)
-        total = squares[rows, :]
-        for j in range(8):
-            part = tok[(m + d + NM) % NM, rows, j * 128:(j + 1) * 128].astype(jnp.float32)
-            total = total + part * part
-        squares[rows, :] = total
-
-    for half in (0, 1):
-        add_squares(0, half)
+        scale = gain[pl.ds(pl.multiple_of(b * 1024, 1024), 1024)].astype(jnp.float32).reshape(1, 1024)
+        column = inverse[rows, 0:1]
+        nrm[b, rows, :] = (tok[b, rows, :].astype(jnp.float32) * column * scale).astype(jnp.bfloat16)
 
     def y_steps():
+        find_inverse()
+        for half in (0, 1):
+            normalise(0, half)
         for k in (1, 2, 3, 4):
             for half in (0, 1):
                 for d in DIST[k]:
@@ -288,7 +334,7 @@
                     way = -1 if d > 0 else 1
                     if k < 3 or (k == 3 and way == (1 if half == 0 else -1)):
                         y_send(d, half, way)
-                    add_squares(d, half)
+                    normalise(d, half)
                     yield
 
     def p_copy(way_k):
@@ -330,60 +376,55 @@
         tables[1] = jnp.where(front, -sines, sines)
 
     def weight_steps():
-        yield from wg.b_arrive(1)
+        yield from wg.b_arrive(2)
         yield from wg.b_across(0)
         yield from wg.a_arrive(1)
         collect_ids()
-        yield from wg.b_arrive(2)
         yield from wg.b_across(1)
+        yield from wg.b_last(0)
+        yield from wg.b_arrive(3)
+        yield from wg.b_arrive(4)
+        yield from wg.b_across(2)
+        yield from wg.b_last(1)
         yield from wg.a_arrive(2)
-        yield from wg.b_arrive(3)
-        yield from wg.b_across(2)
+        yield from wg.b_across(3)
+        yield from wg.b_last(2)
         yield from wg.a_arrive(3)
         make_tables()
-        yield from wg.b_arrive(4)
-        yield from wg.b_across(3)
-        yield from wg.a_arrive(4)
-        yield from wg.b_across(4)
-
-    ring = y_steps()
-    for index, _ in enumerate(weight_steps()):
-        if index >= 4 and index % 5 < 2:
-            next(ring, None)
-    drain(ring)
-
-    inverse = lax.rsqrt(jnp.sum(squares[...], axis=1, keepdims=True) / (NM * 1024.0) + 1e-06)
-    acc[...] = jnp.zeros_like(acc)
-    den[...] = jnp.zeros_like(den)
-    mx[...] = jnp.full(mx.shape, -1e30, jnp.float32)
-    for dz in range(NZ):
-        wg.wait_sib(0, dz)
-        wg.wait_sib(1, dz)
-
     def of_core(block, core):
         cols = [block[:, (k * 2 + core) * T:(k * 2 + core + 1) * T] for k in range(NX)]
         return jnp.concatenate(cols, axis=1)
 
-    def core_rows(b, core):
-        return pl.ds(pl.multiple_of((core * NZ + b) * NX * T, NX * T), NX * T)
-
-    def project_kv(b, total):
-        at = pl.ds(pl.multiple_of(b * 1024, 1024), 1024)
-        scale = gain[at].astype(jnp.float32).reshape(1, 1024)
-        normed = (tok[b].astype(jnp.float32) * inverse * scale).astype(jnp.bfloat16)
-        nrm[b] = normed
+    def project(dz):
+        b = wg.at_z(dz)
+        wg.wait_sib(0, dz)
+        wg.wait_sib(1, dz)
+        normed = nrm[b]
         for core in (0, 1):
-            total = total + jnp.dot(
-                of_core(normed, core), wb[core_rows(b, core), 512 - CA:CB], preferred_element_type=jnp.float32
-            )
-        return total
-
-    linear = lax.fori_loop(0, NM, project_kv, jnp.zeros((T, HD), jnp.float32))
+            rows = pl.ds(pl.multiple_of((core * NZ + b) * NX * T, NX * T), NX * T)
+            part = of_core(normed, core)
+            line_b[...] += jnp.dot(part, wb[rows, :], preferred_element_type=jnp.float32)
+            line_a[...] += jnp.dot(part, wa[rows, :], preferred_element_type=jnp.float32)
+
+    ring = y_steps()
+    for index, _ in enumerate(weight_steps()):
+        if index % 3 == 2:
+            next(ring, None)
+    drain(ring)
+    drain(wg.b_across(4))
+    project(0)
+    drain(wg.b_last(3))
+    project(-1)
+    project(1)
+    drain(wg.a_arrive(4))
+    drain(wg.b_last(4))
+    for dz in (-2, 2, -3, 3, 4):
+        project(dz)
 
     def rotate(part):
         return part * tables[0] + pltpu.roll(part, HD // 2, axis=1) * tables[1]
 
-    linear = linear + jnp.where(is_key, biases[1:2, head_cols], biases[2:3, head_cols])
+    linear = line_b[:, 512 - CA:CB] + jnp.where(is_key, biases[1:2, head_cols], biases[2:3, head_cols])
     own_kind[own, :] = jnp.where(is_key, rotate(linear), linear).astype(jnp.bfloat16)
 
     exchange = pltpu.make_async_remote_copy(
@@ -393,24 +434,13 @@
     exchange.start()
     kg.start_b()
 
-    def project_q(b, carry):
-        qa, qb = carry
-        for core in (0, 1):
-            rows = core_rows(b, core)
-            part = of_core(nrm[b], core)
-            qa = qa + jnp.dot(part, wa[rows, :], preferred_element_type=jnp.float32)
-            qb = qb + jnp.dot(part, wb[rows, 0:512 - CA], preferred_element_type=jnp.float32)
-        return qa, qb
-
-    zeros = jnp.zeros((T, CA), jnp.float32)
-    qa, qb = lax.fori_loop(0, NM, project_q, (zeros, zeros))
+
+    for h in range(4):
+        part = (line_a, line_b)[h // 2][:, (h % 2) * HD:(h % 2 + 1) * HD]
+        qs[h] = rotate(part + biases[0:1, h * HD:(h + 1) * HD]).astype(jnp.bfloat16)
+
     exchange.wait_recv()
     kg.start_a()
-
-    for h in range(4):
-        part = (qa, qb)[h // 2][:, (h % 2) * HD:(h % 2 + 1) * HD]
-        qs[h] = rotate(part + biases[0:1, h * HD:(h + 1) * HD]).astype(jnp.bfloat16)
-
     key_base = jnp.where(is_key, 0, NS * T)
 
     def slab_body(zz, masked):
@@ -471,19 +501,24 @@
     drain(kg.first())
     drain(kg.b_arrive(2))
     drain(kg.b_across(0))
+    drain(kg.b_last(0))
     drain(kg.b_arrive(3))
     drain(kg.a_arrive(1))
     drain(kg.b_arrive(4))
     drain(kg.b_across(1))
+    drain(kg.b_last(1))
     slab(0)
     drain(kg.a_arrive(2))
     drain(kg.b_across(2))
+    drain(kg.b_last(2))
     slab(1)
     drain(kg.a_arrive(3))
     drain(kg.b_across(3))
+    drain(kg.b_last(3))
     slab(2)
     drain(kg.a_arrive(4))
     drain(kg.b_across(4))
+    drain(kg.b_last(4))
     slab(3)
     slab(4)
 
@@ -505,6 +540,10 @@
         @pl.loop(1, NM)
         def _(k):
             p_copy(k).wait_send()
+
+    @pl.loop(1, NM)
+    def _(k):
+        sums_copy(k).wait_send()
 
     exchange.wait_send()
     seven = tok.at[pl.ds(0, 7)]
@@ -557,10 +596,14 @@
             pltpu.VMEM((4, T, HD), jnp.float32),
             pltpu.VMEM((4, T, HD), jnp.float32),
             pltpu.VMEM((4, T, HD), jnp.float32),
-            pltpu.VMEM((T, HD), jnp.float32),
+            pltpu.VMEM((T, CA), jnp.float32),
+            pltpu.VMEM((T, CB), jnp.float32),
+            pltpu.VMEM((T, T), jnp.float32),
+            pltpu.VMEM((8, T), jnp.float32),
+            pltpu.VMEM((NM, 8, T), jnp.float32),
             pltpu.VMEM((2, T, HD), jnp.float32),
             pltpu.VMEM((8, 512), jnp.float32),
-            dma((10,)), dma((1,)), dma((1,)), dma((NZ,)), dma((1,)),
+            dma((10,)), dma((NM,)), dma((1,)), dma((1,)), dma((1,)), dma((NZ,)), dma((1,)),
             dma((1,)), dma((NM, 2)), dma((NM,)), dma((1,)), dma((2,)),
         ] + gather_sems() + gather_sems(),
         compiler_params=pltpu.CompilerParams(

time: 94.7 us -> 89.8 us (0.948)
  Pallas kernels: 93 us -> 88.1 us
    pallas_call x1, Pallas kernels: 93 us -> 88.1 us  [shards(): pl.pallas_call(kernel, name='fused', out_shape=jax.ShapeDtypeStruct((T, 5...]
where the time goes in v3:
time: 89.8 us; the launch traced here: 89.6 us
  Pallas kernels  88.1 us (98%)
  local copies, waits for them, and re-layouts  1.57 us (2%)
    pallas_call x1, Pallas kernels, shards(): pl.pallas_call(kernel, name='fused', out_shape=jax.ShapeDtypeStruct((T, 5...  88.1 us

profile of v3, /device:TPU:1, one launch (start us, length us, event | category | flops | bytes accessed | tf_op | source)
XLA Modules:
  0.0 89.6 jit_solution(16241799510402499098)
XLA Ops:
  0.0 88.1 %fused.1 = bf16[128,512]{1,0:T(8,128)(2,1)} custom-call(bf16[128,1024]{1,0:T(8,128)(2,1)} %frames_in.1, s32[3,128]{1,0:T(4,128)} %bitcast.1, bf16[8192]{0:T(1024)(128)(2,1)} %gain_hbm.1, bf16[128,512]{1,0:T(8,128)(2,1)} %wq.1, bf16[128,512]{1,0:T(8,128)(2,1)} %wk.1, bf16[128,512]{1,0:T(8,128)(2,1)} %wv.1, bf16[512]{0:T(512)(128)(2,1)} %bq_hbm.1, ...), custom_call_target="tpu_custom_call" | custom-call | flops 5000000000 | bytes 10000000 | tf_op jit(solution)/shard_map/fused/pallas_call | solution.py:569
  88.1 1.6 %copy.12 = bf16[128,512]{1,0:T(8,128)(2,1)} copy(bf16[128,512]{1,0:T(8,128)(2,1)} %fused.1) | data formatting | bytes 262144

commit v4 on v3

--- a/solution.py
+++ b/solution.py
@@ -447,8 +447,7 @@
         def rows_of(base, core):
             return pl.ds(pl.multiple_of(base + (core * NZ + zz) * NX * T, NX * T), NX * T)
 
-        @pl.loop(0, 4)
-        def _(h):
+        for h in range(4):
             scores = jnp.concatenate(
                 [
                     lax.dot_general(

time: 89.8 us -> 88.6 us (0.987)
  Pallas kernels: 88.1 us -> 86.9 us
    pallas_call x1, Pallas kernels: 88.1 us -> 86.9 us  [shards(): pl.pallas_call(kernel, name='fused', out_shape=jax.ShapeDtypeStruct((T, 5...]
where the time goes in v4:
time: 88.6 us; the launch traced here: 88.5 us
  Pallas kernels  86.9 us (98%)
  local copies, waits for them, and re-layouts  1.57 us (2%)
    pallas_call x1, Pallas kernels, shards(): pl.pallas_call(kernel, name='fused', out_shape=jax.ShapeDtypeStruct((T, 5...  86.9 us

profile of v4, /device:TPU:1, one launch (start us, length us, event | category | flops | bytes accessed | tf_op | source)
XLA Modules:
  0.0 88.5 jit_solution(17212560266626272023)
XLA Ops:
  0.0 86.9 %fused.1 = bf16[128,512]{1,0:T(8,128)(2,1)} custom-call(bf16[128,1024]{1,0:T(8,128)(2,1)} %frames_in.1, s32[3,128]{1,0:T(4,128)} %bitcast.1, bf16[8192]{0:T(1024)(128)(2,1)} %gain_hbm.1, bf16[128,512]{1,0:T(8,128)(2,1)} %wq.1, bf16[128,512]{1,0:T(8,128)(2,1)} %wk.1, bf16[128,512]{1,0:T(8,128)(2,1)} %wv.1, bf16[512]{0:T(512)(128)(2,1)} %bq_hbm.1, ...), custom_call_target="tpu_custom_call" | custom-call | flops 5000000000 | bytes 10000000 | tf_op jit(solution)/shard_map/fused/pallas_call | solution.py:568
  87.0 1.6 %copy.12 = bf16[128,512]{1,0:T(8,128)(2,1)} copy(bf16[128,512]{1,0:T(8,128)(2,1)} %fused.1) | data formatting | bytes 262144
